TPU v7x, 1024 devices: a whole 8x8x8 slice. The times are simulated.
1024 devices in a mesh: wave: 64 (over z_hi, x, core), lev: 16 (over y, z_lo).
Axes of the slice: x: 8, y: 8, z: 8 (z_hi: 4, z_lo: 2; z = z_hi * 2 + z_lo), core: 2. Of those that a mesh axis runs over, the one named last changes fastest.
Arguments:
- spectral: bfloat16 [320, 2, 64, 641], P('wave', None, 'lev'), may hold values from -6 to 6
- legendre: bfloat16 [320, 641, 640], P('wave'), as said below
- quad_weights: float32 [640], replicated, as said below
- pair_order: int32 [320], replicated, may hold values from 0 to 319, as said below
- lon_counts: int32 [1280], replicated, may hold values from 20 to 2560
- vertical: bfloat16 [64, 64], replicated, may hold values from -0.75 to 0.75
- wind_field: bfloat16 [1280, 64, 2560], P('wave', 'lev'), may hold values from -6 to 6
Outputs:
- spectral_tendency: float32 [320, 2, 64, 641], P('wave', None, 'lev')
Inputs may be any that keep to these rules, and one draw needn't show every extreme that they name: Each pair index appears once; slot s holds the wavenumbers pair_order[s] and 639 - pair_order[s], and the rows of spectral and legendre in slot s follow it. legendre[s, r, j] is the associated Legendre function of row r's degree and wavenumber, normalized so that the integral of its square over mu = cos(colatitude) from -1 to 1 is 1, at the node j of quad_weights; the southern node 1279 - j mirrors node j. `quad_weights`: Positive.
All inputs are finite; a program needn't handle non-finite values.
Results may differ from a plain program's by a relative error of at most 0.0077.
Values may be sent and summed in bfloat16 or wider, within the bound.
A program may use at most 32 MiB of HBM per device.

v0:
```python
import math

import jax
import jax.numpy as jnp
from jax import lax
from jax.experimental import pallas as pl
from jax.experimental.pallas import tpu as pltpu
from jax.sharding import PartitionSpec as P

MESH = pl.DeviceIdType.MESH
F32 = jnp.float32
BF16 = jnp.bfloat16

WAVES = 64
LEVS = 16
SLOTS = 5
LEVELS = 4
TOTAL = 640
BAND = 20
LONS = 2560
HALF = LONS // 2
TILE = 16
COLS = 2 * SLOTS * 2 * WAVES


def dot(a, b):
    return jnp.dot(a, b, preferred_element_type=F32)


def dot_nt(a, b):
    return lax.dot_general(a, b, (((1,), (1,)), ((), ())), preferred_element_type=F32)


def iota(shape, dim):
    return lax.broadcasted_iota(jnp.int32, shape, dim)


def rows_at(start, size=TILE):
    return pl.ds(pl.multiple_of(start, TILE), size)


def half_angle(phase):
    wrapped = phase - float(LONS) * jnp.floor(phase * (1.0 / LONS) + 0.5)
    u = wrapped * (math.pi / LONS)
    q = u * u
    sine = u * (
        1.0
        + q * (-1 / 6 + q * (1 / 120 + q * (-1 / 5040 + q * (1 / 362880 + q * (-1 / 39916800)))))
    )
    cosine = 1.0 + q * (
        -1 / 2
        + q * (1 / 24 + q * (-1 / 720 + q * (1 / 40320 + q * (-1 / 3628800 + q * (1 / 479001600)))))
    )
    return 1.0 - 2.0 * sine * sine, 2.0 * sine * cosine


def group_row(row, half):
    g, rho = (row - 80 * half) // TILE, row % TILE
    last = g == 4
    s = jnp.where(last, 4, (rho // 2) % 4)
    t = rho % 2
    c = jnp.where(last, (rho // 2) % 2, rho // 8)
    level = jnp.where(last, rho // 4, g)
    return 32 * s + 16 * t + 8 * half + 4 * c + level


def kernel(
    spec_ref,
    leg_hbm,
    qw_ref,
    pair_ref,
    cnt_ref,
    vert_ref,
    wind_hbm,
    out_ref,
    leg_v,
    wind_v,
    wind_f,
    mixm,
    s1f,
    s1,
    r1,
    s2,
    r2,
    basis,
    keep_even,
    keep_odd,
    back_even,
    back_odd,
    fb,
    hs,
    sel_out,
    sel_in,
    s3,
    r3,
    xt,
    ff,
    fp,
    bk,
    s5,
    r5,
    dup,
    local_sem,
    send_sem,
    recv_sem,
):
    w = lax.axis_index("wave")
    v = lax.axis_index("lev")
    north = w < WAVES // 2

    barrier = pltpu.get_barrier_semaphore()

    @pl.loop(1, LEVS)
    def _(i):
        pl.semaphore_signal(barrier, 1, device_id={"lev": lax.rem(v + i, LEVS)}, device_id_type=MESH)

    @pl.loop(1, WAVES)
    def _(i):
        pl.semaphore_signal(barrier, 1, device_id={"wave": lax.rem(w + i, WAVES)}, device_id_type=MESH)

    leg_copy = pltpu.make_async_copy(leg_hbm, leg_v, local_sem.at[0])
    leg_copy.start()
    wind_copy = pltpu.make_async_copy(wind_hbm, wind_v, local_sem.at[1])
    wind_copy.start()

    first_lane = iota((LEVELS, 128), 1) == 0

    @pl.loop(0, SLOTS)
    def _(s):
        for chunk in range(6):
            for c in range(2):
                if chunk < 5:
                    piece = spec_ref[s, c, :, 128 * chunk : 128 * chunk + 128].astype(F32)
                else:
                    column = spec_ref[s, c, :, TOTAL : TOTAL + 1].astype(F32)
                    piece = jnp.where(first_lane, jnp.broadcast_to(column, (LEVELS, 128)), 0.0)
                at = 8 * (chunk % 2) + 4 * c
                s1f[3 * s + chunk // 2, at : at + LEVELS, :] = piece

    s1f[15] = jnp.zeros((TILE, 128), F32)
    s1[...] = s1f[...].reshape(256, 128).astype(BF16)

    pick = (iota((256, 64), 1) == 4 * (iota((256, 64), 0) // 16) + iota((256, 64), 0) % 4).astype(BF16)
    spread = dot_nt(dot(pick, vert_ref[...]).astype(BF16), pick)
    same = (iota((256, 256), 0) // 4) % 4 == (iota((256, 256), 1) // 4) % 4
    mixm[...] = jnp.where(same, spread, 0.0).astype(BF16)

    pl.semaphore_wait(barrier, LEVS - 1 + WAVES - 1)

    def lev_send(phase, source, target):
        @pl.loop(1, LEVS)
        def _(i):
            d = lax.rem(v + i, LEVS)
            pltpu.make_async_remote_copy(
                src_ref=source.at[rows_at(TILE * d)],
                dst_ref=target.at[rows_at(TILE * v)],
                send_sem=send_sem.at[phase],
                recv_sem=recv_sem.at[phase],
                device_id={"lev": d},
                device_id_type=MESH,
            ).start()

        pltpu.make_async_copy(
            source.at[rows_at(TILE * v)], target.at[rows_at(TILE * v)], recv_sem.at[phase]
        ).start()

    def all_landed(phase, target):
        pltpu.make_async_copy(target, target, recv_sem.at[phase]).wait()

    def all_sent(phase, source):
        part = source.at[pl.ds(0, source.shape[0] - TILE)]
        pltpu.make_async_copy(part, part, send_sem.at[phase]).wait()

    lane8 = iota((8, 128), 1)
    row8 = iota((8, 128), 0)
    group8 = lane8 // BAND
    lat_of = lane8 % BAND
    counts = jnp.zeros((8, 128), jnp.int32)
    for jj in range(BAND):
        lat = jnp.where(north, BAND * w + jj, BAND * w + BAND - 1 - jj)
        counts = jnp.where(lat_of == jj, cnt_ref[lat], counts)
    counts = jnp.where(group8 < 5, counts, 0)

    def wave_rows(first, stride):
        m = jnp.zeros((8, 128), jnp.int32)
        for i in range(4):
            m = jnp.where(row8 // 2 == i, pair_ref[first + stride * i], m)
        return jnp.where(row8 % 2 == 1, TOTAL - 1 - m, m)

    def make_rows(tile, m):
        mf = m.astype(F32)
        factor = jnp.where(m == 0, 1.0, 2.0)
        cos0, sin0 = half_angle(mf * lane8.astype(F32))
        turn_c, turn_s = half_angle(mf * 128.0)
        real, imag = factor * cos0, -factor * sin0
        for a in range(HALF // 128):
            basis[rows_at(TILE * tile), 128 * a : 128 * a + 128] = jnp.concatenate(
                [real, imag], axis=0
            ).astype(BF16)
            if a + 1 < HALF // 128:
                real, imag = real * turn_c + imag * turn_s, imag * turn_c - real * turn_s
        kept = (2 * m < counts) & (group8 < 4)
        scale = jnp.where(m == 0, 1.0 / LONS, 1.0 / (2 * LONS))
        even = jnp.where(kept & (m % 2 == 0), scale, 0.0)
        odd = jnp.where(kept & (m % 2 == 1), scale, 0.0)
        back_even[rows_at(TILE * tile), :] = jnp.concatenate([even, even], axis=0)
        back_odd[rows_at(TILE * tile), :] = jnp.concatenate([odd, odd], axis=0)

    def prepare(start, stop):
        @pl.loop(start, stop)
        def _(tile):
            m = wave_rows(SLOTS * tile, 1)
            make_rows(tile, m)
            low = pair_ref[SLOTS * tile + 4]
            last = jnp.where(row8 % 2 == 1, TOTAL - 1 - low, low)
            both = jnp.where(group8 < 4, m, last)
            kept = 2 * both < counts
            even = jnp.where(kept & (both % 2 == 0), 1.0, 0.0)
            odd = jnp.where(kept & (both % 2 == 1), 1.0, 0.0)
            keep_even[rows_at(TILE * tile), :] = jnp.concatenate([even, even], axis=0).astype(BF16)
            keep_odd[rows_at(TILE * tile), :] = jnp.concatenate([odd, odd], axis=0).astype(BF16)

    def prepare_last():
        @pl.loop(0, WAVES // 4)
        def _(q):
            make_rows(WAVES + q, wave_rows(4 * SLOTS * q + 4, SLOTS))

    lev_send(0, s1, r1)
    prepare(0, 24)
    row = iota((160, 160), 0)
    column = iota((160, 160), 1)
    sel_out[...] = (column == group_row(row, row // 80)).astype(BF16)
    sel_in[...] = (row == group_row(column, column // 80)).astype(BF16)
    all_landed(0, r1)
    s2[...] = dot(mixm[...], r1[...]).astype(BF16)
    lev_send(1, s2, r2)
    prepare(24, 48)
    dr, dc = iota((1024, 256), 0), iota((1024, 256), 1)
    wanted = 16 * (dr // 64) + 8 * ((dr // 2) % 2) + 2 * ((dr // 16) % 4) + dr % 2
    dup[...] = (dc == wanted).astype(BF16)
    all_landed(1, r2)
    leg_copy.wait()

    for s in range(SLOTS):
        low = pair_ref[SLOTS * w + s]
        pieces = []
        corner = None
        for e in range(3):
            pair_chunk = r2[TILE * (3 * s + e) : TILE * (3 * s + e) + TILE, :].astype(F32)
            for half in range(2):
                a = pair_chunk[8 * half : 8 * half + 8]
                r = lane8 + 128 * (2 * e + half)
                first = r < TOTAL - low
                gap = jnp.where(first, r, r - TOTAL + low)
                sign = jnp.where(gap % 2 == 0, 1.0, -1.0)
                t0 = jnp.where(first, a, 0.0)
                t1 = jnp.where(first, 0.0, a)
                quad = jnp.concatenate([t0, t0 * sign, t1, t1 * sign], axis=0)
                if 2 * e + half < 5:
                    pieces.append(quad.astype(BF16))
                else:
                    corner = quad[:, 0:1]
        coefs = jnp.concatenate(pieces, axis=1)
        last_row = leg_v[s, TOTAL : TOTAL + 1, :].astype(F32)
        total = dot(coefs, leg_v[s, 0:TOTAL, :]) + corner * last_row
        fb[32 * s : 32 * s + 32, :] = total.astype(BF16)

    f = dot(sel_out[...], fb[...])
    lane = iota((32, 768), 1) // BAND % 5
    blank = jnp.zeros((32, 128), F32)
    shifted = []
    for g in range(5):
        part = jnp.concatenate([f[16 * g : 16 * g + 16], f[80 + 16 * g : 96 + 16 * g]], axis=0)
        wide = jnp.concatenate([part, blank], axis=1)
        shifted.append(wide if g == 0 else pltpu.roll(wide, BAND * g, axis=1))
    for beta in range(5):
        merged = shifted[0]
        for g in range(1, 5):
            merged = jnp.where(lane == (g + beta) % 5, shifted[g], merged)
        hs[32 * beta : 32 * beta + 32, :] = merged

    own_north = jnp.where(north, w, WAVES - 1 - w)

    def wave_send(phase, source, target, d):
        pltpu.make_async_remote_copy(
            src_ref=source.at[rows_at(TILE * d)],
            dst_ref=target.at[rows_at(TILE * w)],
            send_sem=send_sem.at[phase],
            recv_sem=recv_sem.at[phase],
            device_id={"wave": d},
            device_id_type=MESH,
        ).start()

    def keep_own(phase, source, target):
        pltpu.make_async_copy(
            source.at[rows_at(TILE * w)], target.at[rows_at(TILE * w)], recv_sem.at[phase]
        ).start()

    def window_of(b):
        start = BAND * b
        aligned = (start // 128) * 128
        return pl.ds(pl.multiple_of(aligned, 128), 256), start - aligned

    def cut(b):
        lanes, offset = window_of(b)
        window = hs[rows_at(32 * lax.rem(b, 5), 32), lanes]
        message = pltpu.roll(window, lax.rem(256 - offset, 256), axis=1)[:, 0:128].astype(BF16)
        s3[rows_at(TILE * b), :] = message[0:16]
        s3[rows_at(TILE * (WAVES - 1 - b)), :] = message[16:32]

    @pl.loop(1, WAVES // 2)
    def _(i):
        b = lax.rem(own_north + i, WAVES // 2)
        cut(b)
        wave_send(2, s3, r3, b)
        wave_send(2, s3, r3, WAVES - 1 - b)

    cut(own_north)
    wave_send(2, s3, r3, WAVES - 1 - w)
    keep_own(2, s3, r3)

    prepare(48, WAVES)
    prepare_last()
    wind_copy.wait()

    @pl.loop(0, BAND // 2)
    def _(q):
        wind_f[q, 0:4, :] = wind_v[2 * q].astype(F32)
        wind_f[q, 4:8, :] = wind_v[2 * q + 1].astype(F32)

    all_landed(2, r3)

    qi = iota((160, 128), 0)
    ql = iota((160, 128), 1)
    lat_row = (qi % 80) // 4
    node = jnp.where(north, lat_row, BAND - 1 - lat_row)
    group = jnp.where(qi < 80, qi % 4, 4)
    gather = (ql == BAND * group + node).astype(BF16)
    level_match = iota((80, 1024), 0) % 4 == (iota((80, 1024), 1) // 4) % 4
    for half, keep in enumerate((keep_even, keep_odd)):
        y = dot_nt(gather, r3[...] * keep[...])
        xt[80 * half : 80 * half + 80, 0:1024] = y[0:80].astype(BF16)
        single = jnp.where(level_match, y[80:160], 0.0).astype(BF16)
        xt[80 * half : 80 * half + 80, 1024:COLS] = dot(single, dup[...]).astype(BF16)

    si = iota((256, 160), 0)
    sj = iota((256, 160), 1)
    half_row = si // 128
    lane_row = si % 128
    lat_nat = jnp.where(north, lane_row % BAND, BAND - 1 - lane_row % BAND)
    wanted_col = 80 * half_row + 4 * lat_nat + lane_row // BAND
    scatter = ((sj == wanted_col) & (lane_row < 80)).astype(BF16)

    @pl.loop(0, HALF // 256)
    def _(j):
        low = pl.ds(pl.multiple_of(256 * j, 256), 256)
        high = pl.ds(pl.multiple_of(HALF + 256 * j, 256), 256)
        g = dot(xt[...], basis[:, low])
        even, odd = g[0:80], g[80:160]
        near = (even + odd).astype(BF16).astype(F32) * wind_f[:, :, low].reshape(80, 256)
        far = (even - odd).astype(BF16).astype(F32) * wind_f[:, :, high].reshape(80, 256)
        ff[0:80, :] = (near + far).astype(BF16)
        ff[80:160, :] = (near - far).astype(BF16)
        fp[:, low] = dot(scatter, ff[...]).astype(BF16)

    @pl.loop(0, COLS // 256)
    def _(j):
        rows = pl.ds(pl.multiple_of(256 * j, 256), 256)
        product = dot_nt(basis[rows, :], fp[...])
        bk[rows, :] = (
            product[:, 0:128] * back_even[rows, :] + product[:, 128:256] * back_odd[rows, :]
        ).astype(BF16)

    zi, zl = iota((1024, 128), 0), iota((1024, 128), 1)
    own_level = (zl // BAND) == (zi // 4) % 4
    fold_r, fold_c = iota((128, 128), 0), iota((128, 128), 1)
    fold = ((fold_c == 80 + fold_r % BAND) & (fold_r < 80)).astype(BF16)
    last_rows = jnp.where(own_level, dot(dup[...], bk[1024:COLS, :]), 0.0).astype(BF16)
    s5[...] = (bk[0:1024, :].astype(F32) + dot(last_rows, fold)).astype(BF16)

    @pl.loop(1, WAVES)
    def _(i):
        wave_send(3, s5, r5, lax.rem(w + i, WAVES))

    keep_own(3, s5, r5)
    hs[...] = jnp.zeros_like(hs)
    all_landed(3, r5)

    empty = jnp.zeros((32, 128), F32)

    @pl.loop(0, WAVES // 2)
    def _(b):
        lanes, offset = window_of(b)
        upper = r5[rows_at(TILE * b), :].astype(F32)
        lower = r5[rows_at(TILE * (WAVES - 1 - b)), :].astype(F32)
        folded = jnp.concatenate([upper + lower, upper - lower], axis=0)
        placed = pltpu.roll(jnp.concatenate([folded, empty], axis=1), offset, axis=1)
        hs[rows_at(32 * lax.rem(b, 5), 32), lanes] += placed

    weights = qw_ref[...]
    for g in range(5):
        merged = hs[0:32, :]
        for beta in range(1, 5):
            merged = jnp.where(lane == (g + beta) % 5, hs[32 * beta : 32 * beta + 32, :], merged)
        if g:
            merged = pltpu.roll(merged, 768 - BAND * g, axis=1)
        merged = (merged[:, 0:TOTAL] * weights).astype(BF16)
        fb[16 * g : 16 * g + 16, :] = merged[0:16]
        fb[80 + 16 * g : 96 + 16 * g, :] = merged[16:32]

    folded_rows = dot(sel_in[...], fb[...]).astype(BF16)
    r_all = iota((8, TOTAL + 1), 1)
    for s in range(SLOTS):
        low = pair_ref[SLOTS * w + s]
        first = r_all < TOTAL - low
        gap = jnp.where(first, r_all, r_all - TOTAL + low)
        odd = gap % 2 == 1
        o = dot_nt(folded_rows[32 * s : 32 * s + 32], leg_v[s])
        result = jnp.where(
            first, jnp.where(odd, o[8:16], o[0:8]), jnp.where(odd, o[24:32], o[16:24])
        )
        out_ref[s, 0] = result[0:4]
        out_ref[s, 1] = result[4:8]

    all_sent(0, s1)
    all_sent(1, s2)
    all_sent(2, s3)
    all_sent(3, s5)


def shards(spectral, legendre, quad_weights, pair_order, lon_counts, vertical, wind_field):
    vmem = pl.BlockSpec(memory_space=pltpu.VMEM)
    smem = pl.BlockSpec(memory_space=pltpu.SMEM)
    hbm = pl.BlockSpec(memory_space=pl.ANY)
    message = pltpu.VMEM((TILE * WAVES, 128), BF16)
    tiles = pltpu.VMEM((TILE * LEVS, 128), BF16)
    return pl.pallas_call(
        kernel,
        out_shape=jax.ShapeDtypeStruct(spectral.shape, F32),
        in_specs=[vmem, hbm, vmem, smem, smem, vmem, hbm],
        out_specs=vmem,
        scratch_shapes=[
            pltpu.VMEM(legendre.shape, BF16),
            pltpu.VMEM(wind_field.shape, BF16),
            pltpu.VMEM((BAND // 2, 8, LONS), F32),
            pltpu.VMEM((256, 256), BF16),
            pltpu.VMEM((LEVS, TILE, 128), F32),
            tiles,
            tiles,
            tiles,
            tiles,
            pltpu.VMEM((COLS, HALF), BF16),
            message,
            message,
            pltpu.VMEM((COLS, 128), F32),
            pltpu.VMEM((COLS, 128), F32),
            pltpu.VMEM((160, TOTAL), BF16),
            pltpu.VMEM((160, 768), F32),
            pltpu.VMEM((160, 160), BF16),
            pltpu.VMEM((160, 160), BF16),
            message,
            message,
            pltpu.VMEM((160, COLS), BF16),
            pltpu.VMEM((160, 256), BF16),
            pltpu.VMEM((256, HALF), BF16),
            pltpu.VMEM((COLS, 128), BF16),
            message,
            message,
            pltpu.VMEM((1024, 256), BF16),
            pltpu.SemaphoreType.DMA((2,)),
            pltpu.SemaphoreType.DMA((4,)),
            pltpu.SemaphoreType.DMA((4,)),
        ],
        compiler_params=pltpu.CompilerParams(
            collective_id=0, has_side_effects=True, vmem_limit_bytes=50 * 1024 * 1024
        ),
    )(
        spectral,
        legendre,
        quad_weights.reshape(1, TOTAL),
        pair_order,
        lon_counts,
        vertical,
        wind_field,
    )


def solution(mesh):
    return jax.shard_map(
        shards,
        mesh=mesh,
        in_specs=(
            P("wave", None, "lev", None),
            P("wave", None, None),
            P(),
            P(),
            P(),
            P(),
            P("wave", "lev", None),
        ),
        out_specs=P("wave", None, "lev", None),
        check_vma=False,
    )
```

profile of v0, /device:TPU:1, one launch (start us, length us, event | category | flops | bytes accessed | tf_op | source)
XLA Modules:
  0.0 70.7 jit_solution(6219501552236543777)
XLA Ops:
  0.0 0.7 reshape.3.qw_ref
  0.7 0.0 copy-start
  0.7 1.0 %copy-done = bf16[20,4,2560]{2,1,0:T(4,128)(2,1)S(1)} copy-done((bf16[20,4,2560]{2,1,0:T(4,128)(2,1)S(1)}, bf16[20,4,2560]{2,1,0:T(4,128)(2,1)}, u32[]{:S(2)}) %copy-start) | copy-done | bytes 409624
  1.7 0.0 copy-start.1
  1.7 0.8 %copy-done.1 = bf16[5,2,4,641]{3,2,1,0:T(4,128)(2,1)S(1)} copy-done((bf16[5,2,4,641]{3,2,1,0:T(4,128)(2,1)S(1)}, bf16[5,2,4,641]{3,2,1,0:T(4,128)(2,1)}, u32[]{:S(2)}) %copy-start.1) | copy-done | bytes 51304
  2.5 0.0 copy-start.2
  2.5 0.7 %copy-done.2 = bf16[64,64]{1,0:T(8,128)(2,1)S(1)} copy-done((bf16[64,64]{1,0:T(8,128)(2,1)S(1)}, bf16[64,64]{1,0:T(8,128)(2,1)}, u32[]{:S(2)}) %copy-start.2) | copy-done | bytes 8216
  3.2 0.0 copy-start.3
  3.2 0.7 copy-done.3
  3.9 0.0 copy-start.4
  3.9 0.7 copy-done.4
  4.6 65.5 %shard_map.73 = f32[5,2,4,641]{3,2,1,0:T(4,128)S(1)} custom-call(bf16[5,2,4,641]{3,2,1,0:T(4,128)(2,1)S(1)} %copy-done.1, bf16[5,641,640]{2,1,0:T(8,128)(2,1)} %leg_hbm.1, f32[1,640]{1,0:T(1,128)S(1)} %reshape.3.qw_ref, s32[320]{0:T(512)S(1)} %copy-done.4, s32[1280]{0:T(1024)S(1)} %copy-done.3, bf16[64,64]{1,0:T(8,128)(2,1)S(1)} %copy-done.2, ...), custom_call_target="tpu_custom_call" | custom-call | tf_op jit(solution)/shard_map/pallas_call | solution.py:437
  70.1 0.7 copy.9
Async XLA Ops:
  0.7 1.0 %copy-start = (bf16[20,4,2560]{2,1,0:T(4,128)(2,1)S(1)}, bf16[20,4,2560]{2,1,0:T(4,128)(2,1)}, u32[]{:S(2)}) copy-start(bf16[20,4,2560]{2,1,0:T(4,128)(2,1)} %wind_hbm.1) | copy-start | bytes 1228804
  1.7 0.8 %copy-start.1 = (bf16[5,2,4,641]{3,2,1,0:T(4,128)(2,1)S(1)}, bf16[5,2,4,641]{3,2,1,0:T(4,128)(2,1)}, u32[]{:S(2)}) copy-start(bf16[5,2,4,641]{3,2,1,0:T(4,128)(2,1)} %spec_ref.1) | copy-start | bytes 153844
  2.5 0.7 %copy-start.2 = (bf16[64,64]{1,0:T(8,128)(2,1)S(1)}, bf16[64,64]{1,0:T(8,128)(2,1)}, u32[]{:S(2)}) copy-start(bf16[64,64]{1,0:T(8,128)(2,1)} %vert_ref.1) | copy-start | bytes 24580
  3.2 0.7 copy-start.3
  3.9 0.7 copy-start.4
where the time goes:
time: 71.1 us; the launch traced here: 70.7 us
  Pallas kernels  65.5 us (92%)
  local copies, waits for them, and re-layouts  5.26 us (7%)
    pallas_call x1, Pallas kernels, shards(): pl.pallas_call(kernel, out_shape=jax.ShapeDtypeStruct(spectral.shape, F32...  65.5 us
    unnamed x11, local copies, waits for them, and re-layouts  4.57 us

commit v1 on v0

v1 whole, which is shorter than its diff:
```python
import math

import jax
import jax.numpy as jnp
from jax import lax
from jax.experimental import pallas as pl
from jax.experimental.pallas import tpu as pltpu
from jax.sharding import PartitionSpec as P

MESH = pl.DeviceIdType.MESH
F32 = jnp.float32
BF16 = jnp.bfloat16

WAVES = 64
LEVS = 16
SLOTS = 5
LEVELS = 4
TOTAL = 640
BAND = 20
LONS = 2560
HALF = LONS // 2
TILE = 16
MIXERS = 13
GROUPS = 4
GROUP_ROWS = TILE * WAVES // GROUPS
COLS = 2 * SLOTS * 2 * WAVES


def dot(a, b):
    return jnp.dot(a, b, preferred_element_type=F32)


def dot_nt(a, b):
    return lax.dot_general(a, b, (((1,), (1,)), ((), ())), preferred_element_type=F32)


def iota(shape, dim):
    return lax.broadcasted_iota(jnp.int32, shape, dim)


def rows_at(start, size=TILE):
    return pl.ds(pl.multiple_of(start, TILE), size)


def half_angle(phase):
    wrapped = phase - float(LONS) * jnp.floor(phase * (1.0 / LONS) + 0.5)
    u = wrapped * (math.pi / LONS)
    q = u * u
    sine = u * (
        1.0
        + q * (-1 / 6 + q * (1 / 120 + q * (-1 / 5040 + q * (1 / 362880 + q * (-1 / 39916800)))))
    )
    cosine = 1.0 + q * (
        -1 / 2
        + q * (1 / 24 + q * (-1 / 720 + q * (1 / 40320 + q * (-1 / 3628800 + q * (1 / 479001600)))))
    )
    return 1.0 - 2.0 * sine * sine, 2.0 * sine * cosine


def group_row(row, half):
    g, rho = (row - 80 * half) // TILE, row % TILE
    last = g == 4
    s = jnp.where(last, 4, (rho // 2) % 4)
    t = rho % 2
    c = jnp.where(last, (rho // 2) % 2, rho // 8)
    level = jnp.where(last, rho // 4, g)
    return 32 * s + 16 * t + 8 * half + 4 * c + level


def kernel(
    spec_hbm,
    leg_hbm,
    qw_hbm,
    pair_hbm,
    cnt_hbm,
    vert_hbm,
    wind_hbm,
    out_ref,
    spec_ref,
    qw_ref,
    pair_ref,
    cnt_ref,
    vert_ref,
    leg_v,
    wind_v,
    wind_f,
    mixm,
    s1f,
    s1,
    r1,
    s2,
    r2,
    basis,
    keep_even,
    keep_odd,
    back_even,
    back_odd,
    fb,
    hs,
    sel_out,
    sel_in,
    s3,
    r3,
    xt,
    acc,
    ff,
    fp,
    s5,
    r5,
    dup,
    dup_one,
    ready,
    local_sem,
    send_sem,
    recv_sem,
):
    w = lax.axis_index("wave")
    v = lax.axis_index("lev")
    north = w < WAVES // 2

    small = (
        (spec_hbm, spec_ref),
        (vert_hbm, vert_ref),
        (pair_hbm, pair_ref),
        (cnt_hbm, cnt_ref),
        (qw_hbm, qw_ref),
    )
    loads = [
        pltpu.make_async_copy(source, target, local_sem.at[2 + i])
        for i, (source, target) in enumerate(small)
    ]
    for copy in loads:
        copy.start()

    barrier = pltpu.get_barrier_semaphore()

    @pl.loop(1, LEVS)
    def _(i):
        pl.semaphore_signal(barrier, 1, device_id={"lev": lax.rem(v + i, LEVS)}, device_id_type=MESH)

    major, minor = w // 8, w % 8

    @pl.loop(1, 8)
    def _(i):
        across = 8 * lax.rem(major + i, 8) + minor
        pl.semaphore_signal(barrier, 1, device_id={"wave": across}, device_id_type=MESH)
        along = 8 * major + lax.rem(minor + i, 8)
        pl.semaphore_signal(barrier, 1, device_id={"wave": along}, device_id_type=MESH)

    for copy in loads:
        copy.wait()
    leg_copy = pltpu.make_async_copy(leg_hbm, leg_v, local_sem.at[0])
    leg_copy.start()
    wind_copy = pltpu.make_async_copy(wind_hbm, wind_v, local_sem.at[1])
    wind_copy.start()

    first_lane = iota((LEVELS, 128), 1)

    @pl.loop(0, SLOTS)
    def _(s):
        for c in range(2):
            for chunk in range(5):
                piece = spec_ref[s, c, :, 128 * chunk : 128 * chunk + 128].astype(F32)
                s1f[5 * s + chunk, 4 * c : 4 * c + 4, :] = piece

    for c in range(2):
        piece = jnp.zeros((LEVELS, 128), F32)
        for s in range(SLOTS):
            column = spec_ref[s, c, :, TOTAL : TOTAL + 1].astype(F32)
            piece = jnp.where(first_lane == s, jnp.broadcast_to(column, (LEVELS, 128)), piece)
        s1f[25, 4 * c : 4 * c + 4, :] = piece
    s1[...] = s1f[...].reshape(TILE * MIXERS, 128).astype(BF16)

    pl.semaphore_wait(barrier, LEVS - 1 + 14)

    def lev_send(phase, source, target, d, here, there):
        pltpu.make_async_remote_copy(
            src_ref=source.at[rows_at(TILE * here)],
            dst_ref=target.at[rows_at(TILE * there)],
            send_sem=send_sem.at[phase],
            recv_sem=recv_sem.at[phase],
            device_id={"lev": d},
            device_id_type=MESH,
        ).start()

    def keep_own(phase, source, target, here, there):
        pltpu.make_async_copy(
            source.at[rows_at(TILE * here)], target.at[rows_at(TILE * there)], recv_sem.at[phase]
        ).start()

    def landed(phase, part):
        pltpu.make_async_copy(part, part, recv_sem.at[phase]).wait()

    def sent(phase, part):
        pltpu.make_async_copy(part, part, send_sem.at[phase]).wait()

    lane8 = iota((8, 128), 1)
    row8 = iota((8, 128), 0)
    group8 = lane8 // BAND
    lat_of = lane8 % BAND
    counts = jnp.zeros((8, 128), jnp.int32)
    for jj in range(BAND):
        lat = jnp.where(north, BAND * w + jj, BAND * w + BAND - 1 - jj)
        counts = jnp.where(lat_of == jj, cnt_ref[lat], counts)
    counts = jnp.where(group8 < 5, counts, 0)

    def wave_rows(first, stride):
        m = jnp.zeros((8, 128), jnp.int32)
        for i in range(4):
            m = jnp.where(row8 // 2 == i, pair_ref[first + stride * i], m)
        return jnp.where(row8 % 2 == 1, TOTAL - 1 - m, m)

    def make_rows(tile, m):
        mf = m.astype(F32)
        factor = jnp.where(m == 0, 1.0, 2.0)
        cos0, sin0 = half_angle(mf * lane8.astype(F32))
        turn_c, turn_s = half_angle(mf * 128.0)
        real, imag = factor * cos0, -factor * sin0
        for a in range(HALF // 128):
            basis[rows_at(TILE * tile), 128 * a : 128 * a + 128] = jnp.concatenate(
                [real, imag], axis=0
            ).astype(BF16)
            if a + 1 < HALF // 128:
                real, imag = real * turn_c + imag * turn_s, imag * turn_c - real * turn_s
        kept = (2 * m < counts) & (group8 < 4)
        scale = jnp.where(m == 0, 1.0 / LONS, 1.0 / (2 * LONS))
        even = jnp.where(kept & (m % 2 == 0), scale, 0.0)
        odd = jnp.where(kept & (m % 2 == 1), scale, 0.0)
        back_even[rows_at(TILE * tile), :] = jnp.concatenate([even, even], axis=0)
        back_odd[rows_at(TILE * tile), :] = jnp.concatenate([odd, odd], axis=0)

    def prepare(start, stop):
        @pl.loop(start, stop)
        def _(tile):
            owner = 4 * lax.rem(tile, TILE) + tile // TILE
            m = wave_rows(SLOTS * owner, 1)
            make_rows(tile, m)
            low = pair_ref[SLOTS * owner + 4]
            last = jnp.where(row8 % 2 == 1, TOTAL - 1 - low, low)
            both = jnp.where(group8 < 4, m, last)
            kept = 2 * both < counts
            even = jnp.where(kept & (both % 2 == 0), 1.0, 0.0)
            odd = jnp.where(kept & (both % 2 == 1), 1.0, 0.0)
            keep_even[rows_at(TILE * tile), :] = jnp.concatenate([even, even], axis=0).astype(BF16)
            keep_odd[rows_at(TILE * tile), :] = jnp.concatenate([odd, odd], axis=0).astype(BF16)

    def prepare_last():
        @pl.loop(0, WAVES // 4)
        def _(q):
            owner = TILE * lax.rem(q, 4) + q // 4
            make_rows(WAVES + q, wave_rows(SLOTS * owner + 4, 4 * SLOTS))

    @pl.loop(0, LEVS)
    def _(i):
        d = lax.rem(v + i, LEVS)

        @pl.when((d < MIXERS) & (d != v))
        def _():
            lev_send(0, s1, r1, d, d, v)

    @pl.when(v < MIXERS)
    def _():
        keep_own(0, s1, r1, v, v)

    pick = (iota((256, 64), 1) == 4 * (iota((256, 64), 0) // 16) + iota((256, 64), 0) % 4).astype(BF16)
    spread = dot_nt(dot(pick, vert_ref[...]).astype(BF16), pick)
    same = (iota((256, 256), 0) // 4) % 4 == (iota((256, 256), 1) // 4) % 4
    mixm[...] = jnp.where(same, spread, 0.0).astype(BF16)

    prepare(0, 24)
    row = iota((160, 160), 0)
    column = iota((160, 160), 1)
    sel_out[...] = (column == group_row(row, row // 80)).astype(BF16)
    sel_in[...] = (row == group_row(column, column // 80)).astype(BF16)

    @pl.when(v < MIXERS)
    def _():
        landed(0, r1)
        s2[...] = dot(mixm[...], r1[...]).astype(BF16)

        @pl.loop(1, LEVS)
        def _(i):
            d = lax.rem(v + i, LEVS)
            lev_send(1, s2, r2, d, d, v)

        keep_own(1, s2, r2, v, v)

    @pl.loop(1, 8)
    def _(i):
        across = 8 * lax.rem(major + i, 8) + minor
        pl.semaphore_signal(ready, 1, device_id={"wave": across}, device_id_type=MESH)

    prepare(24, 48)
    dr, dc = iota((1024, 256), 0), iota((1024, 256), 1)
    wanted = 16 * (dr // 64) + 8 * ((dr // 2) % 2) + 2 * ((dr // 16) % 4) + dr % 2
    dup[...] = (dc == wanted).astype(BF16)
    dup_one[...] = dup[0:256, 0:128]
    landed(1, r2)
    leg_copy.wait()

    for s in range(SLOTS):
        low = pair_ref[SLOTS * w + s]
        pieces = []
        corner = None
        for chunk in range(6):
            if chunk < 5:
                a = r2[40 * s + 8 * chunk : 40 * s + 8 * chunk + 8, :].astype(F32)
            else:
                a = r2[200:208, :].astype(F32)
            r = lane8 + 128 * chunk if chunk < 5 else jnp.full((8, 128), TOTAL, jnp.int32)
            first = r < TOTAL - low
            gap = jnp.where(first, r, r - TOTAL + low)
            sign = jnp.where(gap % 2 == 0, 1.0, -1.0)
            t0 = jnp.where(first, a, 0.0)
            t1 = jnp.where(first, 0.0, a)
            quad = jnp.concatenate([t0, t0 * sign, t1, t1 * sign], axis=0)
            if chunk < 5:
                pieces.append(quad.astype(BF16))
            else:
                corner = quad[:, s : s + 1]
        coefs = jnp.concatenate(pieces, axis=1)
        last_row = leg_v[s, TOTAL : TOTAL + 1, :].astype(F32)
        total = dot(coefs, leg_v[s, 0:TOTAL, :]) + corner * last_row
        fb[32 * s : 32 * s + 32, :] = total.astype(BF16)

    f = dot(sel_out[...], fb[...])
    lane = iota((32, 768), 1) // BAND % 5
    blank = jnp.zeros((32, 128), F32)
    shifted = []
    for g in range(5):
        part = jnp.concatenate([f[16 * g : 16 * g + 16], f[80 + 16 * g : 96 + 16 * g]], axis=0)
        wide = jnp.concatenate([part, blank], axis=1)
        shifted.append(wide if g == 0 else pltpu.roll(wide, BAND * g, axis=1))
    for beta in range(5):
        merged = shifted[0]
        for g in range(1, 5):
            merged = jnp.where(lane == (g + beta) % 5, shifted[g], merged)
        hs[32 * beta : 32 * beta + 32, :] = merged

    def slot_of(device):
        return TILE * lax.rem(device, GROUPS) + device // GROUPS

    group = lax.rem(w, GROUPS)
    own_slot = slot_of(w)

    def wave_send(phase, source, target, k, d):
        pltpu.make_async_remote_copy(
            src_ref=source.at[rows_at(TILE * slot_of(d))],
            dst_ref=target.at[rows_at(TILE * own_slot)],
            send_sem=send_sem.at[phase],
            recv_sem=recv_sem.at[2 + GROUPS * (phase - 2) + k],
            device_id={"wave": d},
            device_id_type=MESH,
        ).start()

    def window_of(b):
        start = BAND * b
        aligned = (start // 128) * 128
        return pl.ds(pl.multiple_of(aligned, 128), 256), start - aligned

    def mirror(band):
        upper = band < WAVES // 2
        return jnp.where(upper, band, WAVES - 1 - band), jnp.where(upper, 0, TILE), upper

    def cut(d):
        b, south, _ = mirror(d)
        lanes, offset = window_of(b)
        window = hs[rows_at(32 * lax.rem(b, 5) + south), lanes]
        message = pltpu.roll(window, lax.rem(256 - offset, 256), axis=1)[:, 0:128].astype(BF16)
        s3[rows_at(TILE * slot_of(d)), :] = message

    def target_of(k, j):
        return lax.rem(group + k, GROUPS) + GROUPS * lax.rem(w // GROUPS + j, TILE)

    pl.semaphore_wait(ready, 7)
    for k in range(GROUPS):

        @pl.loop(0, TILE, unroll=8)
        def _(j):
            cut(target_of(k, j))

        if k == 0:
            keep_own(2, s3, r3, own_slot, own_slot)

        @pl.loop(0 if k else 1, TILE)
        def _(j):
            wave_send(2, s3, r3, k, target_of(k, j))

    prepare(48, WAVES)
    prepare_last()
    wind_copy.wait()

    @pl.loop(0, BAND // 2)
    def _(q):
        wind_f[q, 0:4, :] = wind_v[2 * q].astype(F32)
        wind_f[q, 4:8, :] = wind_v[2 * q + 1].astype(F32)

    qi = iota((160, 128), 0)
    ql = iota((160, 128), 1)
    lat_row = (qi % 80) // 4
    node = jnp.where(north, lat_row, BAND - 1 - lat_row)
    column_of = jnp.where(qi < 80, qi % 4, 4)
    gather = (ql == BAND * column_of + node).astype(BF16)
    level_match = iota((80, 256), 0) % 4 == (iota((80, 256), 1) // 4) % 4
    singles = [jnp.zeros((80, 256), F32)] * 2
    for k in range(GROUPS):
        block = pl.ds(pl.multiple_of(GROUP_ROWS * lax.rem(group - k + GROUPS, GROUPS), GROUP_ROWS), GROUP_ROWS)
        landed(2 + k, r3.at[block])
        for half, keep in enumerate((keep_even, keep_odd)):
            y = dot_nt(gather, r3[block, :] * keep[block, :])
            xt[80 * half : 80 * half + 80, 0:256] = y[0:80].astype(BF16)
            single = jnp.where(level_match, y[80:160], 0.0).astype(BF16)
            singles[half] = singles[half] + dot(single, dup[block, :])
        if k + 1 < GROUPS:

            for j in range(HALF // 256):
                low = pl.ds(256 * j, 256)
                term = dot(xt[:, 0:256], basis[block, low])
                acc[:, low] = acc[:, low] + term if k else term

    for half in range(2):
        xt[80 * half : 80 * half + 80, 256:512] = singles[half].astype(BF16)

    si = iota((256, 160), 0)
    sj = iota((256, 160), 1)
    half_row = si // 128
    lane_row = si % 128
    lat_nat = jnp.where(north, lane_row % BAND, BAND - 1 - lane_row % BAND)
    wanted_col = 80 * half_row + 4 * lat_nat + lane_row // BAND
    scatter = ((sj == wanted_col) & (lane_row < 80)).astype(BF16)

    for j in range(HALF // 256):
        low = pl.ds(256 * j, 256)
        high = pl.ds(HALF + 256 * j, 256)
        g = (
            acc[:, low]
            + dot(xt[:, 0:256], basis[block, low])
            + dot(xt[:, 256:512], basis[1024:COLS, low])
        )
        even, odd = g[0:80], g[80:160]
        near = (even + odd).astype(BF16).astype(F32) * wind_f[:, :, low].reshape(80, 256)
        far = (even - odd).astype(BF16).astype(F32) * wind_f[:, :, high].reshape(80, 256)
        ff[0:80, :] = (near + far).astype(BF16)
        ff[80:160, :] = (near - far).astype(BF16)
        fp[:, low] = dot(scatter, ff[...]).astype(BF16)

    zi, zl = iota((256, 128), 0), iota((256, 128), 1)
    own_level = (zl // BAND) == (zi // 4) % 4
    fold_r, fold_c = iota((128, 128), 0), iota((128, 128), 1)
    fold = ((fold_c == 80 + fold_r % BAND) & (fold_r < 80)).astype(BF16)

    def spectral_rows(rows):
        product = dot_nt(basis[rows, :], fp[...])
        return product[:, 0:128] * back_even[rows, :] + product[:, 128:256] * back_odd[rows, :]

    for k in range(GROUPS):
        target_group = lax.rem(group + k, GROUPS)
        block = pl.ds(pl.multiple_of(GROUP_ROWS * target_group, GROUP_ROWS), GROUP_ROWS)
        main = spectral_rows(block).astype(BF16).astype(F32)
        single = spectral_rows(pl.ds(pl.multiple_of(1024 + 64 * target_group, 64), 64)).astype(BF16)
        spread_rows = jnp.where(own_level, dot(dup_one[:, 0:64], single), 0.0).astype(BF16)
        s5[block, :] = (main + dot(spread_rows, fold)).astype(BF16)
        if k == 0:
            keep_own(6, s5, r5, own_slot, own_slot)

        @pl.loop(0 if k else 1, TILE)
        def _(j):
            wave_send(3, s5, r5, k, target_of(k, j))

    hs[...] = jnp.zeros_like(hs)
    empty = jnp.zeros((TILE, 128), F32)
    for k in range(GROUPS):
        source_group = lax.rem(group - k + GROUPS, GROUPS)
        landed(6 + k, r5.at[rows_at(GROUP_ROWS * source_group, GROUP_ROWS)])

        @pl.loop(0, TILE, unroll=4)
        def _(j):
            b, _, upper = mirror(GROUPS * j + source_group)
            lanes, offset = window_of(b)
            message = r5[rows_at(GROUP_ROWS * source_group + TILE * j), :].astype(F32)
            placed = pltpu.roll(jnp.concatenate([message, empty], axis=1), offset, axis=1)
            at = 32 * lax.rem(b, 5)
            hs[rows_at(at), lanes] += placed
            hs[rows_at(at + TILE), lanes] += placed * jnp.where(upper, 1.0, -1.0)

    weights = qw_ref[...].reshape(1, TOTAL)
    for g in range(5):
        merged = hs[0:32, :]
        for beta in range(1, 5):
            merged = jnp.where(lane == (g + beta) % 5, hs[32 * beta : 32 * beta + 32, :], merged)
        if g:
            merged = pltpu.roll(merged, 768 - BAND * g, axis=1)
        merged = (merged[:, 0:TOTAL] * weights).astype(BF16)
        fb[16 * g : 16 * g + 16, :] = merged[0:16]
        fb[80 + 16 * g : 96 + 16 * g, :] = merged[16:32]

    folded_rows = dot(sel_in[...], fb[...]).astype(BF16)
    r_all = iota((8, TOTAL + 1), 1)
    for s in range(SLOTS):
        low = pair_ref[SLOTS * w + s]
        first = r_all < TOTAL - low
        gap = jnp.where(first, r_all, r_all - TOTAL + low)
        odd = gap % 2 == 1
        o = dot_nt(folded_rows[32 * s : 32 * s + 32], leg_v[s])
        result = jnp.where(
            first, jnp.where(odd, o[8:16], o[0:8]), jnp.where(odd, o[24:32], o[16:24])
        )
        out_ref[s, 0] = result[0:4]
        out_ref[s, 1] = result[4:8]

    @pl.when(v < MIXERS)
    def _():
        sent(0, s1.at[pl.ds(0, TILE * (MIXERS - 1))])
        sent(1, s2.at[pl.ds(0, TILE * (LEVS - 1))])

    @pl.when(v >= MIXERS)
    def _():
        sent(0, s1)

    sent(2, s3.at[pl.ds(0, TILE * (WAVES - 1))])
    sent(3, s5.at[pl.ds(0, TILE * (WAVES - 1))])


def shards(spectral, legendre, quad_weights, pair_order, lon_counts, vertical, wind_field):
    vmem = pl.BlockSpec(memory_space=pltpu.VMEM)
    hbm = pl.BlockSpec(memory_space=pltpu.HBM)
    message = pltpu.VMEM((TILE * WAVES, 128), BF16)
    tiles = pltpu.VMEM((TILE * LEVS, 128), BF16)
    return pl.pallas_call(
        kernel,
        out_shape=jax.ShapeDtypeStruct(spectral.shape, F32),
        in_specs=[hbm] * 7,
        out_specs=vmem,
        scratch_shapes=[
            pltpu.VMEM(spectral.shape, BF16),
            pltpu.VMEM(quad_weights.shape, F32),
            pltpu.SMEM(pair_order.shape, jnp.int32),
            pltpu.SMEM(lon_counts.shape, jnp.int32),
            pltpu.VMEM(vertical.shape, BF16),
            pltpu.VMEM(legendre.shape, BF16),
            pltpu.VMEM(wind_field.shape, BF16),
            pltpu.VMEM((BAND // 2, 8, LONS), F32),
            pltpu.VMEM((256, 256), BF16),
            pltpu.VMEM((2 * MIXERS, 8, 128), F32),
            pltpu.VMEM((TILE * MIXERS, 128), BF16),
            tiles,
            tiles,
            pltpu.VMEM((TILE * MIXERS, 128), BF16),
            pltpu.VMEM((COLS, HALF), BF16),
            message,
            message,
            pltpu.VMEM((COLS, 128), F32),
            pltpu.VMEM((COLS, 128), F32),
            pltpu.VMEM((160, TOTAL), BF16),
            pltpu.VMEM((160, 768), F32),
            pltpu.VMEM((160, 160), BF16),
            pltpu.VMEM((160, 160), BF16),
            message,
            message,
            pltpu.VMEM((160, 512), BF16),
            pltpu.VMEM((160, HALF), F32),
            pltpu.VMEM((160, 256), BF16),
            pltpu.VMEM((256, HALF), BF16),
            message,
            message,
            pltpu.VMEM((1024, 256), BF16),
            pltpu.VMEM((256, 128), BF16),
            pltpu.SemaphoreType.REGULAR,
            pltpu.SemaphoreType.DMA((7,)),
            pltpu.SemaphoreType.DMA((4,)),
            pltpu.SemaphoreType.DMA((10,)),
        ],
        compiler_params=pltpu.CompilerParams(
            collective_id=0, has_side_effects=True, vmem_limit_bytes=63 * 1024 * 1024
        ),
    )(
        spectral,
        legendre,
        quad_weights,
        pair_order,
        lon_counts,
        vertical,
        wind_field,
    )


def solution(mesh):
    return jax.shard_map(
        shards,
        mesh=mesh,
        in_specs=(
            P("wave", None, "lev", None),
            P("wave", None, None),
            P(),
            P(),
            P(),
            P(),
            P("wave", "lev", None),
        ),
        out_specs=P("wave", None, "lev", None),
        check_vma=False,
    )
```

time: 71.1 us -> 63.7 us (0.90)
  local copies, waits for them, and re-layouts: 5.26 us -> 1.56 us
  Pallas kernels: 65.5 us -> 61.9 us
    pallas_call x1, Pallas kernels: 65.5 us -> 61.9 us  [shards(): pl.pallas_call(kernel, out_shape=jax.ShapeDtypeStruct(spectral.shape, F32...]
    unnamed x11 -> x1, local copies, waits for them, and re-layouts: 4.57 us -> 1.56 us
where the time goes in v1:
time: 63.7 us; the launch traced here: 63.5 us
  Pallas kernels  61.9 us (97%)
  local copies, waits for them, and re-layouts  1.56 us (2%)
    pallas_call x1, Pallas kernels, shards(): pl.pallas_call(kernel, out_shape=jax.ShapeDtypeStruct(spectral.shape, F32...  61.9 us
    unnamed x1, local copies, waits for them, and re-layouts  1.56 us

profile of v1, /device:TPU:1, one launch (start us, length us, event | category | flops | bytes accessed | tf_op | source)
XLA Modules:
  0.0 63.5 jit_solution(4297494750209165762)
XLA Ops:
  0.0 61.9 %shard_map.73 = f32[5,2,4,641]{3,2,1,0:T(4,128)} custom-call(bf16[5,2,4,641]{3,2,1,0:T(4,128)(2,1)} %spec_hbm.1, bf16[5,641,640]{2,1,0:T(8,128)(2,1)} %leg_hbm.1, f32[640]{0:T(1024)} %qw_hbm.1, s32[320]{0:T(512)} %pair_hbm.1, s32[1280]{0:T(1024)} %cnt_hbm.1, bf16[64,64]{1,0:T(8,128)(2,1)} %vert_hbm.1, bf16[20,4,2560]{2,1,0:T(4,128)(2,1)} %wind_hbm.1), custom_call_target="tpu_custom_call" | custom-call | tf_op jit(solution)/shard_map/pallas_call | solution.py:529
  62.0 1.6 %copy.9 = f32[5,2,4,641]{3,2,1,0:T(4,128)} copy(f32[5,2,4,641]{3,2,1,0:T(4,128)} %shard_map.73) | data formatting | bytes 205120

commit v2 on v1

--- a/solution.py
+++ b/solution.py
@@ -22,6 +22,7 @@
 TILE = 16
 MIXERS = 13
 GROUPS = 4
+ORDER = (2, 1, 3, 0)
 GROUP_ROWS = TILE * WAVES // GROUPS
 COLS = 2 * SLOTS * 2 * WAVES
 
@@ -173,6 +174,12 @@
 
     pl.semaphore_wait(barrier, LEVS - 1 + 14)
 
+    def far_first(i):
+        return 4 + ((i + 1) // 2) * (1 - 2 * lax.rem(i, 2))
+
+    def lev_target(i):
+        return 2 * lax.rem(v // 2 + far_first(i // 2), 8) + lax.rem(v + i + 1, 2)
+
     def lev_send(phase, source, target, d, here, there):
         pltpu.make_async_remote_copy(
             src_ref=source.at[rows_at(TILE * here)],
@@ -232,10 +239,9 @@
     def prepare(start, stop):
         @pl.loop(start, stop)
         def _(tile):
-            owner = 4 * lax.rem(tile, TILE) + tile // TILE
-            m = wave_rows(SLOTS * owner, 1)
+            m = wave_rows(SLOTS * tile, 1)
             make_rows(tile, m)
-            low = pair_ref[SLOTS * owner + 4]
+            low = pair_ref[SLOTS * tile + 4]
             last = jnp.where(row8 % 2 == 1, TOTAL - 1 - low, low)
             both = jnp.where(group8 < 4, m, last)
             kept = 2 * both < counts
@@ -247,14 +253,13 @@
     def prepare_last():
         @pl.loop(0, WAVES // 4)
         def _(q):
-            owner = TILE * lax.rem(q, 4) + q // 4
-            make_rows(WAVES + q, wave_rows(SLOTS * owner + 4, 4 * SLOTS))
-
-    @pl.loop(0, LEVS)
+            make_rows(WAVES + q, wave_rows(4 * SLOTS * q + 4, SLOTS))
+
+    @pl.loop(0, LEVS - 1)
     def _(i):
-        d = lax.rem(v + i, LEVS)
-
-        @pl.when((d < MIXERS) & (d != v))
+        d = lev_target(i)
+
+        @pl.when(d < MIXERS)
         def _():
             lev_send(0, s1, r1, d, d, v)
 
@@ -278,9 +283,9 @@
         landed(0, r1)
         s2[...] = dot(mixm[...], r1[...]).astype(BF16)
 
-        @pl.loop(1, LEVS)
+        @pl.loop(0, LEVS - 1)
         def _(i):
-            d = lax.rem(v + i, LEVS)
+            d = lev_target(i)
             lev_send(1, s2, r2, d, d, v)
 
         keep_own(1, s2, r2, v, v)
@@ -337,16 +342,13 @@
             merged = jnp.where(lane == (g + beta) % 5, shifted[g], merged)
         hs[32 * beta : 32 * beta + 32, :] = merged
 
-    def slot_of(device):
-        return TILE * lax.rem(device, GROUPS) + device // GROUPS
-
-    group = lax.rem(w, GROUPS)
-    own_slot = slot_of(w)
+    group = w // TILE
+    chip, core = lax.rem(w, TILE) // 2, lax.rem(w, 2)
 
     def wave_send(phase, source, target, k, d):
         pltpu.make_async_remote_copy(
-            src_ref=source.at[rows_at(TILE * slot_of(d))],
-            dst_ref=target.at[rows_at(TILE * own_slot)],
+            src_ref=source.at[rows_at(TILE * d)],
+            dst_ref=target.at[rows_at(TILE * w)],
             send_sem=send_sem.at[phase],
             recv_sem=recv_sem.at[2 + GROUPS * (phase - 2) + k],
             device_id={"wave": d},
@@ -367,10 +369,26 @@
         lanes, offset = window_of(b)
         window = hs[rows_at(32 * lax.rem(b, 5) + south), lanes]
         message = pltpu.roll(window, lax.rem(256 - offset, 256), axis=1)[:, 0:128].astype(BF16)
-        s3[rows_at(TILE * slot_of(d)), :] = message
+        s3[rows_at(TILE * d), :] = message
 
     def target_of(k, j):
-        return lax.rem(group + k, GROUPS) + GROUPS * lax.rem(w // GROUPS + j, TILE)
+        return (
+            TILE * lax.rem(group + ORDER[k], GROUPS)
+            + 2 * lax.rem(chip + far_first(j // 2), 8)
+            + lax.rem(core + j, 2)
+        )
+
+    def send_group(phase, source, target, k):
+        @pl.loop(0, TILE if k + 1 < GROUPS else TILE - 2)
+        def _(j):
+            wave_send(phase, source, target, k, target_of(k, j))
+
+        if k + 1 == GROUPS:
+            wave_send(phase, source, target, k, target_of(k, TILE - 1))
+            keep_own(2 + GROUPS * (phase - 2) + k, source, target, w, w)
+
+    def source_group(k):
+        return lax.rem(group - ORDER[k] + GROUPS, GROUPS)
 
     pl.semaphore_wait(ready, 7)
     for k in range(GROUPS):
@@ -379,12 +397,7 @@
         def _(j):
             cut(target_of(k, j))
 
-        if k == 0:
-            keep_own(2, s3, r3, own_slot, own_slot)
-
-        @pl.loop(0 if k else 1, TILE)
-        def _(j):
-            wave_send(2, s3, r3, k, target_of(k, j))
+        send_group(2, s3, r3, k)
 
     prepare(48, WAVES)
     prepare_last()
@@ -404,7 +417,7 @@
     level_match = iota((80, 256), 0) % 4 == (iota((80, 256), 1) // 4) % 4
     singles = [jnp.zeros((80, 256), F32)] * 2
     for k in range(GROUPS):
-        block = pl.ds(pl.multiple_of(GROUP_ROWS * lax.rem(group - k + GROUPS, GROUPS), GROUP_ROWS), GROUP_ROWS)
+        block = pl.ds(pl.multiple_of(GROUP_ROWS * source_group(k), GROUP_ROWS), GROUP_ROWS)
         landed(2 + k, r3.at[block])
         for half, keep in enumerate((keep_even, keep_odd)):
             y = dot_nt(gather, r3[block, :] * keep[block, :])
@@ -454,30 +467,25 @@
         return product[:, 0:128] * back_even[rows, :] + product[:, 128:256] * back_odd[rows, :]
 
     for k in range(GROUPS):
-        target_group = lax.rem(group + k, GROUPS)
+        target_group = lax.rem(group + ORDER[k], GROUPS)
         block = pl.ds(pl.multiple_of(GROUP_ROWS * target_group, GROUP_ROWS), GROUP_ROWS)
         main = spectral_rows(block).astype(BF16).astype(F32)
         single = spectral_rows(pl.ds(pl.multiple_of(1024 + 64 * target_group, 64), 64)).astype(BF16)
         spread_rows = jnp.where(own_level, dot(dup_one[:, 0:64], single), 0.0).astype(BF16)
         s5[block, :] = (main + dot(spread_rows, fold)).astype(BF16)
-        if k == 0:
-            keep_own(6, s5, r5, own_slot, own_slot)
-
-        @pl.loop(0 if k else 1, TILE)
-        def _(j):
-            wave_send(3, s5, r5, k, target_of(k, j))
+        send_group(3, s5, r5, k)
 
     hs[...] = jnp.zeros_like(hs)
     empty = jnp.zeros((TILE, 128), F32)
     for k in range(GROUPS):
-        source_group = lax.rem(group - k + GROUPS, GROUPS)
-        landed(6 + k, r5.at[rows_at(GROUP_ROWS * source_group, GROUP_ROWS)])
+        first_band = TILE * source_group(k)
+        landed(6 + k, r5.at[rows_at(TILE * first_band, GROUP_ROWS)])
 
         @pl.loop(0, TILE, unroll=4)
         def _(j):
-            b, _, upper = mirror(GROUPS * j + source_group)
+            b, _, upper = mirror(first_band + j)
             lanes, offset = window_of(b)
-            message = r5[rows_at(GROUP_ROWS * source_group + TILE * j), :].astype(F32)
+            message = r5[rows_at(TILE * (first_band + j)), :].astype(F32)
             placed = pltpu.roll(jnp.concatenate([message, empty], axis=1), offset, axis=1)
             at = 32 * lax.rem(b, 5)
             hs[rows_at(at), lanes] += placed
@@ -522,6 +530,7 @@
 
 
 def shards(spectral, legendre, quad_weights, pair_order, lon_counts, vertical, wind_field):
+    operands = (spectral, legendre, quad_weights, pair_order, lon_counts, vertical, wind_field)
     vmem = pl.BlockSpec(memory_space=pltpu.VMEM)
     hbm = pl.BlockSpec(memory_space=pltpu.HBM)
     message = pltpu.VMEM((TILE * WAVES, 128), BF16)
@@ -529,7 +538,7 @@
     return pl.pallas_call(
         kernel,
         out_shape=jax.ShapeDtypeStruct(spectral.shape, F32),
-        in_specs=[hbm] * 7,
+        in_specs=[hbm] * len(operands),
         out_specs=vmem,
         scratch_shapes=[
             pltpu.VMEM(spectral.shape, BF16),
@@ -571,17 +580,9 @@
             pltpu.SemaphoreType.DMA((10,)),
         ],
         compiler_params=pltpu.CompilerParams(
-            collective_id=0, has_side_effects=True, vmem_limit_bytes=63 * 1024 * 1024
+            collective_id=0, has_side_effects=True, vmem_limit_bytes=50 * 1024 * 1024
         ),
-    )(
-        spectral,
-        legendre,
-        quad_weights,
-        pair_order,
-        lon_counts,
-        vertical,
-        wind_field,
-    )
+    )(*(pltpu.with_memory_space_constraint(x, pltpu.HBM) for x in operands))
 
 
 def solution(mesh):

time: 63.7 us -> 63 us (0.989)
  local copies, waits for them, and re-layouts: 1.56 us -> 0.65 us
    unnamed x1, local copies, waits for them, and re-layouts: 1.56 us -> 0.65 us
where the time goes in v2:
time: 63 us; the launch traced here: 62.8 us
  Pallas kernels  62.1 us (99%)
  local copies, waits for them, and re-layouts  0.65 us (1%)
    pallas_call x1, Pallas kernels, shards(): pl.pallas_call(kernel, out_shape=jax.ShapeDtypeStruct(spectral.shape, F32...  62.1 us

profile of v2, /device:TPU:1, one launch (start us, length us, event | category | flops | bytes accessed | tf_op | source)
XLA Modules:
  0.0 62.8 jit_solution(8749124221139407733)
XLA Ops:
  0.0 62.1 %shard_map.73 = f32[5,2,4,641]{3,2,1,0:T(4,128)S(1)} custom-call(bf16[5,2,4,641]{3,2,1,0:T(4,128)(2,1)} %spec_hbm.1, bf16[5,641,640]{2,1,0:T(8,128)(2,1)} %leg_hbm.1, f32[640]{0:T(1024)} %qw_hbm.1, s32[320]{0:T(512)} %pair_hbm.1, s32[1280]{0:T(1024)} %cnt_hbm.1, bf16[64,64]{1,0:T(8,128)(2,1)} %vert_hbm.1, bf16[20,4,2560]{2,1,0:T(4,128)(2,1)} %wind_hbm.1), custom_call_target="tpu_custom_call" | custom-call | tf_op jit(solution)/shard_map/pallas_call | solution.py:538
  62.1 0.7 %copy.9 = f32[5,2,4,641]{3,2,1,0:T(4,128)} copy(f32[5,2,4,641]{3,2,1,0:T(4,128)S(1)} %shard_map.73) | data formatting | bytes 205120

commit v3 on v2

--- a/solution.py
+++ b/solution.py
@@ -135,13 +135,13 @@
 
     barrier = pltpu.get_barrier_semaphore()
 
-    @pl.loop(1, LEVS)
+    @pl.loop(1, LEVS, unroll=True)
     def _(i):
         pl.semaphore_signal(barrier, 1, device_id={"lev": lax.rem(v + i, LEVS)}, device_id_type=MESH)
 
     major, minor = w // 8, w % 8
 
-    @pl.loop(1, 8)
+    @pl.loop(1, 8, unroll=True)
     def _(i):
         across = 8 * lax.rem(major + i, 8) + minor
         pl.semaphore_signal(barrier, 1, device_id={"wave": across}, device_id_type=MESH)
@@ -255,7 +255,7 @@
         def _(q):
             make_rows(WAVES + q, wave_rows(4 * SLOTS * q + 4, SLOTS))
 
-    @pl.loop(0, LEVS - 1)
+    @pl.loop(0, LEVS - 1, unroll=True)
     def _(i):
         d = lev_target(i)
 
@@ -283,14 +283,14 @@
         landed(0, r1)
         s2[...] = dot(mixm[...], r1[...]).astype(BF16)
 
-        @pl.loop(0, LEVS - 1)
+        @pl.loop(0, LEVS - 1, unroll=True)
         def _(i):
             d = lev_target(i)
             lev_send(1, s2, r2, d, d, v)
 
         keep_own(1, s2, r2, v, v)
 
-    @pl.loop(1, 8)
+    @pl.loop(1, 8, unroll=True)
     def _(i):
         across = 8 * lax.rem(major + i, 8) + minor
         pl.semaphore_signal(ready, 1, device_id={"wave": across}, device_id_type=MESH)
@@ -379,7 +379,7 @@
         )
 
     def send_group(phase, source, target, k):
-        @pl.loop(0, TILE if k + 1 < GROUPS else TILE - 2)
+        @pl.loop(0, TILE if k + 1 < GROUPS else TILE - 2, unroll=True)
         def _(j):
             wave_send(phase, source, target, k, target_of(k, j))
 
@@ -393,7 +393,7 @@
     pl.semaphore_wait(ready, 7)
     for k in range(GROUPS):
 
-        @pl.loop(0, TILE, unroll=8)
+        @pl.loop(0, TILE, unroll=True)
         def _(j):
             cut(target_of(k, j))
 
@@ -481,7 +481,7 @@
         first_band = TILE * source_group(k)
         landed(6 + k, r5.at[rows_at(TILE * first_band, GROUP_ROWS)])
 
-        @pl.loop(0, TILE, unroll=4)
+        @pl.loop(0, TILE, unroll=8)
         def _(j):
             b, _, upper = mirror(first_band + j)
             lanes, offset = window_of(b)

time: 63 us -> 60.8 us (0.965)
  Pallas kernels: 62.1 us -> 59.9 us
    pallas_call x1, Pallas kernels: 62.1 us -> 59.9 us  [shards(): pl.pallas_call(kernel, out_shape=jax.ShapeDtypeStruct(spectral.shape, F32...]
where the time goes in v3:
time: 60.8 us; the launch traced here: 60.6 us
  Pallas kernels  59.9 us (99%)
  local copies, waits for them, and re-layouts  0.65 us (1%)
    pallas_call x1, Pallas kernels, shards(): pl.pallas_call(kernel, out_shape=jax.ShapeDtypeStruct(spectral.shape, F32...  59.9 us

profile of v3, /device:TPU:1, one launch (start us, length us, event | category | flops | bytes accessed | tf_op | source)
XLA Modules:
  0.0 60.6 jit_solution(14157943741551369285)
XLA Ops:
  0.0 59.9 %shard_map.73 = f32[5,2,4,641]{3,2,1,0:T(4,128)S(1)} custom-call(bf16[5,2,4,641]{3,2,1,0:T(4,128)(2,1)} %spec_hbm.1, bf16[5,641,640]{2,1,0:T(8,128)(2,1)} %leg_hbm.1, f32[640]{0:T(1024)} %qw_hbm.1, s32[320]{0:T(512)} %pair_hbm.1, s32[1280]{0:T(1024)} %cnt_hbm.1, bf16[64,64]{1,0:T(8,128)(2,1)} %vert_hbm.1, bf16[20,4,2560]{2,1,0:T(4,128)(2,1)} %wind_hbm.1), custom_call_target="tpu_custom_call" | custom-call | tf_op jit(solution)/shard_map/pallas_call | solution.py:538
  59.9 0.7 %copy.9 = f32[5,2,4,641]{3,2,1,0:T(4,128)} copy(f32[5,2,4,641]{3,2,1,0:T(4,128)S(1)} %shard_map.73) | data formatting | bytes 205120
